TPU v7x, 32 devices: a whole 2x2x4 slice. The times are simulated.
32 devices in a mesh: copies: 2 (over y), task: 4 (over z), ops: 4 (over x, core).
Axes of the slice: x: 2, y: 2, z: 4, core: 2. Of those that a mesh axis runs over, the one named last changes fastest.
Arguments:
- psi: bfloat16 [6144, 384], P(('copies', 'task', 'ops')), parts along dimension 0, may hold values from -6 to 6
- left_env: bfloat16 [8, 4, 32, 256, 256], P(('copies', 'ops'), 'task'), parts along dimension 0, may hold values from -0.375 to 0.375
- right_env: bfloat16 [8, 8, 128, 128], P(('copies', 'ops')), parts along dimension 0, may hold values from -0.09375 to 0.09375
- sec_tiles: int32 [8, 4], P('copies'), parts along dimension 0, may hold values from 1 to 2, as said below
- task_sector: int32 [8, 32], P('copies'), parts along dimension 0, may hold values from 0 to 3, as said below
- task_term: int32 [8, 32], P('copies'), parts along dimension 0, may hold values from 0 to 7, as said below
- task_live: int32 [8, 4, 32], P(('copies', 'ops')), parts along dimension 0, may hold values 0 or 1
Outputs:
- sigma: bfloat16 [6144, 384], P(('copies', 'task', 'ops')), parts along dimension 0
There are 2 independent parts, one for each index of `copies`. A program takes and returns all parts, laid end to end along the dimension named above; each array names one. Nothing has to cross between parts.
Inputs may be any that keep to these rules, and one draw needn't show every extreme that they name: `sec_tiles`: each sector owner's 4 sector sizes sum to 6 tiles. `task_sector`: slot k of every task owner holds a task on a sector of sector owner k mod 4; over all task owners and slots, every (sector owner, sector, term) triple with term below 8 appears in exactly one slot. `task_term`: term of each slot, as described for task_sector.
All inputs are finite; a program needn't handle non-finite values. No bound on the sum of `task_live` on one device may be relied on, other than what follows from the above.
Results may differ from a plain program's by a relative error of at most 0.0058.
Values may be sent and summed in bfloat16 or wider, within the bound.
A program may use at most 64 MiB of HBM per device.

v0:
```python
import jax
import jax.numpy as jnp
from jax import lax
from jax.sharding import PartitionSpec as P

TILE = 128
MR = 128
NV = 3


def lookup(entries, selected):
    sector_marks = selected[..., None] == jnp.arange(entries.shape[-1])
    return jnp.sum(jnp.where(sector_marks, entries, 0), axis=-1)


def apply_terms(blocks, pieces, pattern, keep_rows, term_ids, live_flags, right_blocks):
    mixed_rows = jnp.einsum(pattern, blocks, pieces, preferred_element_type=jnp.float32)
    mixed_rows = jnp.where(keep_rows[..., None], mixed_rows, 0.0).astype(jnp.bfloat16)
    leading = mixed_rows.shape[:3]
    per_vector = mixed_rows.reshape(leading + (NV, MR))
    chosen = right_blocks[term_ids]
    result = jnp.einsum("abrvm,abmn->abrvn", per_vector, chosen, preferred_element_type=jnp.float32)
    result = result * live_flags[:, :, None, None, None].astype(jnp.float32)
    return result.reshape(leading + (NV * MR,)).astype(jnp.bfloat16)


def body(psi, left_env, right_env, sec_tiles, task_sector, task_term, task_live):
    owners = lax.axis_size("task")
    owner_index = lax.axis_index("task")
    columns = psi.shape[1]
    span_rows = left_env.shape[-1]
    slot_count = task_sector.shape[1]
    pair_count = slot_count // owners
    sector_count = sec_tiles.shape[1]
    own_block = lax.all_gather(psi, "ops", axis=0, tiled=True)
    own_rows = own_block.shape[0]
    sector_rows = lax.dynamic_index_in_dim(sec_tiles, owner_index, 0, keepdims=False) * TILE
    starts = jnp.cumsum(sector_rows) - sector_rows
    padded = jnp.concatenate([own_block, jnp.zeros((span_rows, columns), own_block.dtype)], axis=0)
    offsets = jnp.arange(span_rows)
    sent_sector = lax.dynamic_index_in_dim(
        task_sector.reshape(owners, pair_count, owners), owner_index, 2, keepdims=False
    )
    counts = lookup(sector_rows, sent_sector)
    begins = lookup(starts, sent_sector)
    send_keep = offsets < counts[..., None]
    row_ids = begins[..., None] + offsets
    pieces = jnp.where(send_keep[..., None], padded[row_ids], jnp.zeros((), own_block.dtype))
    group_live = task_live[0]
    right_blocks = right_env[0]
    arrived = lax.all_to_all(pieces, "task", split_axis=0, concat_axis=0, tiled=True)
    my_sectors = lax.dynamic_index_in_dim(task_sector, owner_index, 0, keepdims=False).reshape(
        pair_count, owners
    )
    all_rows = sec_tiles * TILE
    slot_rows = lookup(all_rows[None, :, :], my_sectors)
    own_keep = offsets < slot_rows[..., None]
    term_ids = lax.dynamic_index_in_dim(task_term, owner_index, 0, keepdims=False).reshape(
        pair_count, owners
    )
    live_flags = lax.dynamic_index_in_dim(group_live, owner_index, 0, keepdims=False).reshape(
        pair_count, owners
    )
    blocks = left_env.reshape(pair_count, owners, span_rows, span_rows)
    result = apply_terms(
        blocks, arrived, "tirs,itsc->tirc", own_keep, term_ids, live_flags, right_blocks
    )
    returned = lax.all_to_all(result, "task", split_axis=1, concat_axis=1, tiled=True)
    sum_pattern = "jtl,tjrc->lrc"
    sector_marks = (sent_sector[..., None] == jnp.arange(sector_count)).astype(jnp.bfloat16)
    sector_sums = jnp.einsum(
        sum_pattern, sector_marks, returned, preferred_element_type=jnp.float32
    )
    placed = jnp.zeros((own_rows + span_rows, columns), jnp.float32)
    for sector in range(sector_count):
        placed = lax.dynamic_update_slice_in_dim(placed, sector_sums[sector], starts[sector], 0)
    summed = lax.psum_scatter(placed[:own_rows], "ops", scatter_dimension=0, tiled=True)
    return summed.astype(jnp.bfloat16)


def solution(mesh):
    return jax.shard_map(
        body,
        mesh=mesh,
        in_specs=(
            P(("copies", "task", "ops"), None),
            P(("copies", "ops"), "task", None, None, None),
            P(("copies", "ops"), None, None, None),
            P("copies", None),
            P("copies", None),
            P("copies", None),
            P(("copies", "ops"), None, None),
        ),
        out_specs=P(("copies", "task", "ops"), None),
        check_vma=False,
    )
```

profile of v0, /device:TPU:0, one launch (start us, length us, event | category | flops | bytes accessed | tf_op | source)
XLA Modules:
  0.0 423.1 jit_solution(11756919224115751606)
XLA Ops:
  6.5 0.7 fusion.13
  7.3 0.2 reduce-window.9
  7.4 0.7 bitcast_subtract_fusion
  8.1 0.8 reshape.115
  8.9 0.2 dynamic-slice_reduce_fusion
  9.1 0.1 select_reduce_fusion.1
  9.3 9.2 %all_gather.3 = bf16[768,384]{1,0:T(8,128)(2,1)S(1)} all-gather(bf16[192,384]{1,0:T(8,128)(2,1)} %param.7), channel_id=1, replica_groups=mesh['copies'=2,'task'=4,'ops'=4] {'ops'}, dimensions={0}, use_global_device_ids=true | all-gather | bytes 737280 | tf_op jit(solution)/shard_map/all_gather | solution.py:35
  18.7 33.1 %gather_fusion = bf16[8192,384]{1,0:T(8,128)(2,1)} fusion(bf16[1024,384]{1,0:T(8,128)(2,1)S(1)} %concatenate.3, s32[8192]{0:T(1024)S(1)} %broadcast_clamp_fusion), kind=kCustom, calls=%fused_computation | custom fusion | bytes 12615680 | tf_op jit(solution)/shard_map/gather | solution.py:48
  51.8 6.3 %broadcast_select_fusion = bf16[4,8,256,384]{3,2,1,0:T(8,128)(2,1)} fusion(bf16[4,8,256,384]{3,2,1,0:T(8,128)(2,1)} %bitcast.56, pred[4,8,256]{2,1,0:T(8,128)(4,1)S(1)} %iota_compare_fusion), kind=kLoop, calls=%fused_computation.6 | loop fusion | flops 3145728 | bytes 12591104 | tf_op jit(solution)/shard_map/jit(_where)/select_n | solution.py:48
  58.1 8.7 %copy.23 = bf16[4,8,256,384]{2,3,1,0:T(8,128)(2,1)} copy(bf16[4,8,256,384]{3,2,1,0:T(8,128)(2,1)} %broadcast_select_fusion) | data formatting | bytes 12582912 | tf_op jit(solution)/shard_map/jit(_where)/select_n | solution.py:48
  66.8 5.4 %all-to-all-start = ((bf16[4,8,256,384]{2,3,1,0:T(8,128)(2,1)}), bf16[4,8,256,384]{2,3,1,0:T(8,128)(2,1)}, u32[]{:S(2)}, u32[]{:S(2)}) async-start(bf16[4,8,256,384]{2,3,1,0:T(8,128)(2,1)} %copy.23), calls=%async_computation | async-start | bytes 12582912 | tf_op jit(solution)/shard_map/all_to_all | solution.py:51
  72.1 0.7 fusion.8
  73.0 0.1 select_reduce_fusion.2
  73.4 0.7 fusion.12
  74.2 1.7 gather_fusion.1
  76.0 135.1 %all-to-all-done = bf16[4,8,256,384]{2,3,1,0:T(8,128)(2,1)} async-done(((bf16[4,8,256,384]{2,3,1,0:T(8,128)(2,1)}), bf16[4,8,256,384]{2,3,1,0:T(8,128)(2,1)}, u32[]{:S(2)}, u32[]{:S(2)}) %all-to-all-start) | async-done | bytes 6291488 | tf_op jit(solution)/shard_map/all_to_all | solution.py:51
  211.1 5.8 %select_convert_fusion = bf16[8,4,384,256]{3,2,1,0:T(8,128)(2,1)S(1)} fusion(pred[8,4,256]{2,1,0:T(4,128)(4,1)S(1)} %iota_compare_fusion.1, bf16[8,4,256,256]{3,2,1,0:T(8,128)(2,1)} %bitcast.65, bf16[4,8,256,384]{2,3,1,0:T(8,128)(2,1)} %all-to-all-done), kind=kOutput, calls=%fused_computation.3 | convolution fusion | flops 1616904192 | bytes 16785408 | tf_op jit(solution)/shard_map/tirs,itsc->tirc/dot_general | solution.py:17
  216.9 6.0 %multiply_convert_fusion = bf16[8,4,256,3,128]{2,4,3,1,0:T(8,128)(2,1)} fusion(f32[8,4]{1,0:T(8,128)S(1)} %convert_element_type.30, bf16[8,4,256,3,128]{2,4,3,1,0:T(8,128)(2,1)S(1)} %bitcast.58, bf16[8,4,128,128,1]{3,2,4,1,0:T(8,128)(2,1)} %bitcast.59), kind=kOutput, calls=%fused_computation.2 | convolution fusion | flops 811597824 | bytes 13631616 | tf_op jit(solution)/shard_map/abrvm,abmn->abrvn/dot_general | solution.py:22
  222.9 9.0 %copy.27 = bf16[8,4,256,384]{3,0,2,1:T(8,128)(2,1)} copy(bf16[8,4,256,384]{2,3,1,0:T(8,128)(2,1)} %bitcast.57) | data formatting | bytes 12582912 | tf_op jit(solution)/shard_map/convert_element_type | solution.py:24
  231.9 5.2 %all-to-all-start.1 = ((bf16[8,4,256,384]{3,0,2,1:T(8,128)(2,1)}), bf16[8,4,256,384]{3,0,2,1:T(8,128)(2,1)}, u32[]{:S(2)}, u32[]{:S(2)}) async-start(bf16[8,4,256,384]{3,0,2,1:T(8,128)(2,1)} %copy.27), calls=%async_computation.1 | async-start | bytes 12582912 | tf_op jit(solution)/shard_map/all_to_all | solution.py:68
  237.2 0.7 fusion.16
  245.5 129.8 %all-to-all-done.1 = bf16[8,4,256,384]{3,0,2,1:T(8,128)(2,1)} async-done(((bf16[8,4,256,384]{3,0,2,1:T(8,128)(2,1)}), bf16[8,4,256,384]{3,0,2,1:T(8,128)(2,1)}, u32[]{:S(2)}, u32[]{:S(2)}) %all-to-all-start.1) | async-done | bytes 6291488 | tf_op jit(solution)/shard_map/all_to_all | solution.py:68
  375.3 4.2 convolution_bitcast_fusion
  379.5 1.2 fusion.15
  380.8 0.1 broadcast_in_dim.70
  380.9 2.0 dynamic_update_slice.12
  382.9 2.0 dynamic_update_slice.13
  384.9 2.0 dynamic_update_slice.14
  386.9 2.0 dynamic_update_slice.15
  388.9 1.1 slice.44
  390.0 24.6 %reduce-scatter.2.cloned.1.call-done = f32[192,384]{1,0:T(8,128)} async-done(((f32[768,384]{1,0:T(8,128)}), f32[192,384]{1,0:T(8,128)}) %reduce-scatter.2.cloned.1.call-update) | async-done | bytes 294928 | tf_op jit(solution)/shard_map/reduce_scatter | solution.py:77
  414.6 1.6 convert_element_type.33
  (25 shorter events, 1.0 us)
Async XLA Ops:
  6.5 67.7 %copy-start = (bf16[1,8,128,128]{3,2,1,0:T(8,128)(2,1)S(1)}, bf16[1,8,128,128]{3,2,1,0:T(8,128)(2,1)}, u32[]{:S(2)}) copy-start(bf16[1,8,128,128]{3,2,1,0:T(8,128)(2,1)} %param.9) | copy-start | bytes 786436
  66.8 6.3 %copy-start.1 = (s32[4,4]{1,0:T(4,128)S(1)}, s32[4,4]{1,0:T(4,128)}, u32[]{:S(2)}) copy-start(s32[4,4]{1,0:T(4,128)} %param.10) | copy-start | bytes 196
  66.8 144.3 %all-to-all-start = ((bf16[4,8,256,384]{2,3,1,0:T(8,128)(2,1)}), bf16[4,8,256,384]{2,3,1,0:T(8,128)(2,1)}, u32[]{:S(2)}, u32[]{:S(2)}) async-start(bf16[4,8,256,384]{2,3,1,0:T(8,128)(2,1)} %copy.23), calls=%async_computation | async-start | bytes 12582912 | tf_op jit(solution)/shard_map/all_to_all | solution.py:51
  231.9 143.4 %all-to-all-start.1 = ((bf16[8,4,256,384]{3,0,2,1:T(8,128)(2,1)}), bf16[8,4,256,384]{3,0,2,1:T(8,128)(2,1)}, u32[]{:S(2)}, u32[]{:S(2)}) async-start(bf16[8,4,256,384]{3,0,2,1:T(8,128)(2,1)} %copy.27), calls=%async_computation.1 | async-start | bytes 12582912 | tf_op jit(solution)/shard_map/all_to_all | solution.py:68
  237.1 177.5 %reduce-scatter.2.cloned.1.call-start = ((), (), s32[]{:S(2)}) async-start(), calls=%async_computation.3 | async-start | bytes 1474560 | tf_op jit(solution)/shard_map/reduce_scatter | solution.py:77
Sparse Core Ops, SparseCore 0:
  390.1 24.4 reduce-scatter.1
where the time goes:
time: 424 us; the launch traced here: 423 us
  waiting for transfers between devices  289 us (68%)
  local copies, waits for them, and re-layouts  65.9 us (16%)
  between operations  21.2 us (5%)
  matrix products  16 us (4%)
  other arithmetic  10.7 us (3%)
  starting transfers between devices  10.6 us (2%)
  blocking collectives  9.19 us (2%)
    all_to_all x1, waiting for transfers between devices, body(): lax.all_to_all(pieces, 'task', split_axis=0, concat_axis=0, tiled=True)  135 us
    all_to_all x1, waiting for transfers between devices, body(): lax.all_to_all(result, 'task', split_axis=1, concat_axis=1, tiled=True)  130 us
    gather x1, local copies, waits for them, and re-layouts, body(): padded[row_ids]  33.1 us
    reduce_scatter x1, waiting for transfers between devices, body(): lax.psum_scatter(placed[:own_rows], 'ops', scatter_dimension=0, tiled=True)  24.6 us
    all_gather x1, blocking collectives, body(): own_block = lax.all_gather(psi, 'ops', axis=0, tiled=True)  9.19 us
    convert_element_type x1, local copies, waits for them, and re-layouts, apply_terms(): return result.reshape(leading + (NV * MR,)).astype(jnp.bfloat16)  8.98 us
    select_n x1, local copies, waits for them, and re-layouts, body(): jnp.where(send_keep[..., None], padded[row_ids], jnp.zeros((), own_block....  8.66 us
  transfers between devices with their start and end apart: 3, of which 3 were waited for; matrix products, arithmetic and copies ran while one was open for 1% of the time, Pallas kernels for 0%

commit v1 on v0

--- a/solution.py
+++ b/solution.py
@@ -1,6 +1,11 @@
+import functools
+import math
+
 import jax
 import jax.numpy as jnp
 from jax import lax
+from jax.experimental import pallas as pl
+from jax.experimental.pallas import tpu as pltpu
 from jax.sharding import PartitionSpec as P
 
 TILE = 128
@@ -78,9 +83,339 @@
     return summed.astype(jnp.bfloat16)
 
 
+MESH = pl.DeviceIdType.MESH
+VMEM_LIMIT = 32 * 1024 * 1024
+
+
+def place():
+    z = lax.axis_index("task")
+    o = lax.axis_index("ops")
+    across = lax.rem(o + 2, 4)
+    sibling = o + 1 - 2 * lax.rem(o, 2)
+    return z, o, across, sibling
+
+
+def enter(z, across, sibling, depth):
+    barrier = pltpu.get_barrier_semaphore()
+
+    def greet(**where):
+        pl.semaphore_signal(barrier, inc=1, device_id=where, device_id_type=MESH)
+
+    greet(ops=across)
+    greet(ops=sibling)
+
+    @pl.when(z > 0)
+    def _():
+        greet(task=z - 1)
+
+    @pl.when(z < depth - 1)
+    def _():
+        greet(task=z + 1)
+
+    inner = jnp.where(z > 0, 1, 0) + jnp.where(z < depth - 1, 1, 0)
+    pl.semaphore_wait(barrier, 2 + inner)
+
+
+def whole_kernel(depth, psi_ref, env_ref, right_ref, tiles_ref, sector_ref, term_ref, live_ref, out_ref, *scratch):
+    steps = 2 * depth - 1
+    homes, scratch = scratch[:steps], scratch[steps:]
+    (env, right, tiles, sector, term, live, first_tile, end_tile, mixed, part, core_buf, side_buf, up_buf, down_buf,
+     side_out, z_out, send_sem, recv_sem, local_sem, core_send, side_send, z_send,
+     core_recv, side_recv, up_recv, down_recv) = scratch
+    z, o, across, sibling = place()
+    other = lax.rem(sibling + 2, 4)
+    pairs = env.shape[0]
+    units, unit = psi_ref.shape[:2]
+    rows = units * unit
+    per_tile = TILE // unit
+    own_tiles = homes[0].shape[0] // per_tile
+    sectors = tiles.shape[1]
+    up, down, side, core = 0, 1, 2, 3
+
+    def block(step, col):
+        return homes[step + depth - 1].at[pl.ds(col * units, units)]
+
+    loads = [
+        pltpu.make_async_copy(source, target, local_sem.at[i])
+        for i, (source, target) in enumerate((
+            (psi_ref, block(0, o)), (tiles_ref, tiles), (sector_ref, sector), (term_ref, term), (live_ref, live),
+            (right_ref, right), (env_ref, env),
+        ))
+    ]
+    for load in loads:
+        load.start()
+    enter(z, across, sibling, depth)
+
+    def copy(way, step, col):
+        shift = (-1, 1, 0, 0)[way]
+        where = ({"task": z + 1}, {"task": z - 1}, {"ops": across}, {"ops": sibling})[way]
+        index = (z + step) * 4 + col
+        own = step == 0 and col is o
+        return pltpu.make_async_remote_copy(
+            src_ref=psi_ref if own else block(step, col),
+            dst_ref=block(step + shift, col),
+            send_sem=send_sem.at[way, index],
+            recv_sem=recv_sem.at[index],
+            device_id=where,
+            device_id_type=MESH,
+        )
+
+    def arrived(step, col):
+        copy(core, step, col).wait_recv()
+
+    def offsets(t):
+        return ((-t, z - t >= 0), (t, z + t <= depth - 1))
+
+    def core_copy(at, far):
+        col = other if far else sibling
+        return pltpu.make_async_remote_copy(
+            src_ref=part.at[at, pl.ds(pl.multiple_of(col * rows, 16), rows)],
+            dst_ref=core_buf.at[int(far), at],
+            send_sem=core_send.at[int(far), at],
+            recv_sem=core_recv.at[int(far), at],
+            device_id={"ops": sibling},
+            device_id_type=MESH,
+        )
+
+    def side_copy(at):
+        return pltpu.make_async_remote_copy(
+            src_ref=side_out.at[at],
+            dst_ref=side_buf.at[at],
+            send_sem=side_send.at[at],
+            recv_sem=side_recv.at[at],
+            device_id={"ops": across},
+            device_id_type=MESH,
+        )
+
+    def z_copy(at, rising):
+        return pltpu.make_async_remote_copy(
+            src_ref=z_out.at[at],
+            dst_ref=(up_buf if rising else down_buf).at[at],
+            send_sem=z_send.at[at],
+            recv_sem=(up_recv if rising else down_recv).at[at],
+            device_id={"task": z + 1 if rising else z - 1},
+            device_id_type=MESH,
+        )
+
+    def wide(value):
+        return value.astype(jnp.float32)
+
+    def part_rows(at, col):
+        return wide(part[at, pl.ds(pl.multiple_of(col * rows, 16), rows), :])
+
+    def apply_home(step):
+        home = z + step
+        held = homes[step + depth - 1]
+
+        def one_slot(pair, _):
+            slot = pair * depth + home
+            which = sector[z, slot]
+            start = jnp.int32(0)
+            for earlier in range(sectors - 1):
+                start += jnp.where(earlier < which, tiles[home, earlier], 0)
+            count = tiles[home, which]
+            first_tile[pair] = start
+            end_tile[pair] = jnp.where(live[0, z, slot] != 0, start + count, start)
+            next_tile = jnp.minimum(start + 1, own_tiles - 1)
+            pieces = [held[start * per_tile + i] for i in range(per_tile)]
+            for i in range(per_tile):
+                piece = held[next_tile * per_tile + i]
+                pieces.append(jnp.where(count > 1, piece, jnp.zeros_like(piece)))
+            rows_in = jnp.concatenate(pieces, axis=0)
+            turned = jnp.dot(env[pair, home], rows_in, preferred_element_type=jnp.float32).astype(jnp.bfloat16)
+            chosen = right[term[z, slot]]
+            for v in range(NV):
+                cols = slice(v * MR, (v + 1) * MR)
+                result = jnp.dot(
+                    turned[:, cols], chosen, preferred_element_type=jnp.float32
+                ).astype(jnp.bfloat16)
+                mixed[pair, 0, :, cols] = result[:TILE]
+                mixed[pair, 1, :, cols] = result[TILE:]
+            return 0
+
+        lax.fori_loop(0, pairs, one_slot, 0, unroll=UNROLL)
+
+        def one_tile(tile, _):
+            for v in range(NV):
+                cols = slice(v * MR, (v + 1) * MR)
+                total = jnp.zeros((TILE, MR), jnp.float32)
+                for pair in range(pairs):
+                    start, end = first_tile[pair], end_tile[pair]
+                    weight = jnp.where((tile >= start) & (tile < end), 1.0, 0.0)
+                    offset = jnp.where(tile > start, 1, 0)
+                    total += weight * wide(mixed[pair, offset, :, cols])
+                part[home, pl.ds(pl.multiple_of(tile * TILE, TILE), TILE), cols] = total.astype(jnp.bfloat16)
+            return 0
+
+        lax.fori_loop(0, own_tiles, one_tile, 0)
+        core_copy(home, True).start()
+        core_copy(home, False).start()
+
+    def finish_home(step):
+        arrived(step, across)
+        copy(core, step, across).start()
+        arrived(step, sibling)
+        arrived(step, other)
+        apply_home(step)
+
+    def send_side(at):
+        core_copy(at, True).wait_recv()
+        side_out[at] = (part_rows(at, across) + wide(core_buf[1, at])).astype(jnp.bfloat16)
+        side_copy(at).start()
+
+    def gathered(at):
+        core_copy(at, False).wait_recv()
+        side_copy(at).wait_recv()
+        return part_rows(at, o) + wide(core_buf[0, at]) + wide(side_buf[at])
+
+    def send_z(step):
+        at = z + step
+        rising = step > 0
+        buf = up_buf if rising else down_buf
+        first = (z == 0) if rising else (z == depth - 1)
+
+        @pl.when(first)
+        def _():
+            z_out[at] = gathered(at).astype(jnp.bfloat16)
+
+        @pl.when(jnp.logical_not(first))
+        def _():
+            total = gathered(at)
+            z_copy(at, rising).wait_recv()
+            z_out[at] = (total + wide(buf[at])).astype(jnp.bfloat16)
+
+        z_copy(at, rising).start()
+
+    @pl.when(z < depth - 1)
+    def _():
+        copy(up, 0, o).start()
+
+    @pl.when(z > 0)
+    def _():
+        copy(down, 0, o).start()
+
+    copy(side, 0, o).start()
+    copy(core, 0, o).start()
+
+    def forward(t):
+        for step, there in offsets(t):
+            @pl.when(there)
+            def _():
+                arrived(step, o)
+
+                if 1 - depth < step < 0:
+                    @pl.when(z < depth - 1)
+                    def _():
+                        copy(up, step, o).start()
+                if 0 < step < depth - 1:
+                    @pl.when(z > 0)
+                    def _():
+                        copy(down, step, o).start()
+
+                copy(side, step, o).start()
+                copy(core, step, o).start()
+
+    forward(1)
+    for load in loads:
+        load.wait()
+    finish_home(0)
+    for t in range(1, depth):
+        if t + 1 < depth:
+            forward(t + 1)
+        if t + 1 == depth - 1:
+            send_side(z)
+        for step, there in offsets(t):
+            pl.when(there)(functools.partial(finish_home, step))
+    if depth < 3:
+        send_side(z)
+
+    order = []
+    for t in range(depth - 1, 0, -1):
+        order += offsets(t)[::-1]
+    for step, there in order:
+        pl.when(there)(functools.partial(send_side, z + step))
+    for step, there in order:
+        pl.when(there)(functools.partial(send_z, step))
+
+    total = gathered(z)
+
+    @pl.when(z == 0)
+    def _():
+        z_copy(z, False).wait_recv()
+        out_ref[...] = (total + wide(down_buf[z])).astype(jnp.bfloat16)
+
+    @pl.when(z == depth - 1)
+    def _():
+        z_copy(z, True).wait_recv()
+        out_ref[...] = (total + wide(up_buf[z])).astype(jnp.bfloat16)
+
+    @pl.when((z > 0) & (z < depth - 1))
+    def _():
+        z_copy(z, True).wait_recv()
+        z_copy(z, False).wait_recv()
+        out_ref[...] = (total + wide(up_buf[z]) + wide(down_buf[z])).astype(jnp.bfloat16)
+
+    def drain(step):
+        at = z + step
+        core_copy(at, True).wait_send()
+        core_copy(at, False).wait_send()
+        side_copy(at).wait_send()
+        copy(side, step, o).wait_send()
+        copy(core, step, o).wait_send()
+        copy(core, step, across).wait_send()
+        if step != 0:
+            z_copy(at, step > 0).wait_send()
+        if 1 - depth < step <= 0:
+            @pl.when(z < depth - 1)
+            def _():
+                copy(up, step, o).wait_send()
+        if 0 <= step < depth - 1:
+            @pl.when(z > 0)
+            def _():
+                copy(down, step, o).wait_send()
+
+    drain(0)
+    for step, there in order:
+        pl.when(there)(functools.partial(drain, step))
+
+
+UNROLL = 2
+
+
+def small_body(psi, left_env, right_env, sec_tiles, task_sector, task_term, task_live):
+    depth = lax.axis_size("task")
+    span = left_env.shape[-1]
+    rows, columns = psi.shape
+    env = left_env.reshape(-1, depth, span, span)
+    right = right_env[0]
+    pairs = env.shape[0]
+    unit = math.gcd(rows, TILE)
+    operands = (psi.reshape(-1, unit, columns), env, right, sec_tiles, task_sector, task_term, task_live)
+    dma, vmem, smem = pltpu.SemaphoreType.DMA, pltpu.VMEM, pltpu.SMEM
+    blocks = vmem((depth, rows, columns), jnp.bfloat16)
+    ints = [smem(a.shape, jnp.int32) for a in operands[3:]]
+    return pl.pallas_call(
+        functools.partial(whole_kernel, depth),
+        out_shape=jax.ShapeDtypeStruct(psi.shape, jnp.bfloat16),
+        in_specs=[pl.BlockSpec(memory_space=pltpu.HBM)] * len(operands),
+        out_specs=pl.BlockSpec(memory_space=pltpu.VMEM),
+        scratch_shapes=[vmem((4 * rows // unit, unit, columns), jnp.bfloat16)] * (2 * depth - 1)
+        + [vmem(env.shape, env.dtype), vmem(right.shape, right.dtype)] + ints
+        + [smem((pairs,), jnp.int32)] * 2
+        + [vmem((pairs, span // TILE, TILE, columns), jnp.bfloat16), vmem((depth, 4 * rows, columns), jnp.bfloat16),
+           vmem((2, depth, rows, columns), jnp.bfloat16)] + [blocks] * 5
+        + [dma((4, depth * 4)), dma((depth * 4,)), dma((len(operands),)), dma((2, depth)), dma((depth,)),
+           dma((depth,)), dma((2, depth)), dma((depth,)), dma((depth,)), dma((depth,))],
+        compiler_params=pltpu.CompilerParams(
+            collective_id=0, has_side_effects=True, vmem_limit_bytes=VMEM_LIMIT
+        ),
+    )(*operands)
+
+
 def solution(mesh):
+    paired = mesh.shape["ops"] == 4 and mesh.shape["task"] <= 4
     return jax.shard_map(
-        body,
+        small_body if paired else body,
         mesh=mesh,
         in_specs=(
             P(("copies", "task", "ops"), None),

time: 424 us -> 58.2 us (0.14)
  waiting for transfers between devices: 289 us -> 0 us
  local copies, waits for them, and re-layouts: 65.9 us -> 7.43 us
  Pallas kernels: 0 us -> 50.2 us
  between operations: 21.2 us -> 0.02 us
  matrix products: 16 us -> 0 us
  other arithmetic: 10.7 us -> 0 us
  starting transfers between devices: 10.6 us -> 0 us
  blocking collectives: 9.19 us -> 0 us
    all_to_all x2 -> x0, waiting for transfers between devices: 265 us -> none  [the longest x1 135 us: body(): lax.all_to_all(pieces, 'task', split_axis=0, concat_axis=0, tiled=True)]
    pallas_call x0 -> x1, Pallas kernels: none -> 50.2 us  [small_body(): pl.pallas_call(functools.partial(whole_kernel, depth), out_shape=jax.Shap...]
    gather x2 -> x0, local copies, waits for them, and re-layouts: 34.9 us -> none  [the longest x1 33.1 us: body(): padded[row_ids]]
    reduce_scatter x1 -> x0, waiting for transfers between devices: 24.6 us -> none  [body(): lax.psum_scatter(placed[:own_rows], 'ops', scatter_dimension=0, tiled=True)]
    dot_general x3 -> x0, matrix products: 16 us -> none  [the longest x1 6 us: apply_terms(): jnp.einsum('abrvm,abmn->abrvn', per_vector, chosen, preferred_element_typ...]
    all_to_all x2 -> x0, starting transfers between devices: 10.6 us -> none  [the longest x1 5.36 us: body(): lax.all_to_all(pieces, 'task', split_axis=0, concat_axis=0, tiled=True)]
    all_gather x1 -> x0, blocking collectives: 9.19 us -> none  [body(): own_block = lax.all_gather(psi, 'ops', axis=0, tiled=True)]
    convert_element_type x2 -> x0, local copies, waits for them, and re-layouts: 9.06 us -> none  [the longest x1 8.98 us: apply_terms(): return result.reshape(leading + (NV * MR,)).astype(jnp.bfloat16)]
  transfers between devices with their start and end apart: 3 -> 0, of which waited for: 3 -> 0; matrix products, arithmetic and copies ran while one was open for 1% -> 0% of each run, Pallas kernels for 0% -> 0%
where the time goes in v1:
time: 58.2 us; the launch traced here: 57.7 us
  Pallas kernels  50.2 us (86%)
  local copies, waits for them, and re-layouts  7.43 us (13%)
    pallas_call x1, Pallas kernels, small_body(): pl.pallas_call(functools.partial(whole_kernel, depth), out_shape=jax.Shap...  50.2 us
    unnamed x15, local copies, waits for them, and re-layouts  7.43 us

profile of v1, /device:TPU:0, one launch (start us, length us, event | category | flops | bytes accessed | tf_op | source)
XLA Modules:
  0.0 57.7 jit_solution(14159601133895510708)
XLA Ops:
  0.0 0.0 copy-start
  0.0 2.2 %copy-done = bf16[1,1,32,256,256]{4,3,2,1,0:T(8,128)(2,1)S(1)} copy-done((bf16[1,1,32,256,256]{4,3,2,1,0:T(8,128)(2,1)S(1)}, bf16[1,1,32,256,256]{4,3,2,1,0:T(8,128)(2,1)}, u32[]{:S(2)}) %copy-start) | copy-done | bytes 4194328
  2.2 0.0 copy-start.1
  2.2 0.9 %copy-done.1 = bf16[1,8,128,128]{3,2,1,0:T(8,128)(2,1)S(1)} copy-done((bf16[1,8,128,128]{3,2,1,0:T(8,128)(2,1)S(1)}, bf16[1,8,128,128]{3,2,1,0:T(8,128)(2,1)}, u32[]{:S(2)}) %copy-start.1) | copy-done | bytes 262168
  3.1 0.0 copy-start.2
  3.1 0.9 %copy-done.2 = bf16[192,384]{1,0:T(8,128)(2,1)S(1)} copy-done((bf16[192,384]{1,0:T(8,128)(2,1)S(1)}, bf16[192,384]{1,0:T(8,128)(2,1)}, u32[]{:S(2)}) %copy-start.2) | copy-done | bytes 147480
  4.0 0.0 copy-start.3
  4.1 0.7 %copy-done.3 = s32[4,4]{1,0:T(4,128)S(1)} copy-done((s32[4,4]{1,0:T(4,128)S(1)}, s32[4,4]{1,0:T(4,128)}, u32[]{:S(2)}) %copy-start.3) | copy-done | bytes 88
  4.7 0.0 copy-start.4
  4.7 0.7 %copy-done.4 = s32[4,32]{1,0:T(4,128)S(1)} copy-done((s32[4,32]{1,0:T(4,128)S(1)}, s32[4,32]{1,0:T(4,128)}, u32[]{:S(2)}) %copy-start.4) | copy-done | bytes 536
  5.4 0.0 copy-start.5
  5.4 0.7 %copy-done.5 = s32[4,32]{1,0:T(4,128)S(1)} copy-done((s32[4,32]{1,0:T(4,128)S(1)}, s32[4,32]{1,0:T(4,128)}, u32[]{:S(2)}) %copy-start.5) | copy-done | bytes 536
  6.1 0.0 copy-start.6
  6.1 0.7 %copy-done.6 = s32[1,4,32]{2,1,0:T(4,128)S(1)} copy-done((s32[1,4,32]{2,1,0:T(4,128)S(1)}, s32[1,4,32]{2,1,0:T(4,128)}, u32[]{:S(2)}) %copy-start.6) | copy-done | bytes 536
  6.8 50.2 %shard_map.73 = bf16[192,384]{1,0:T(8,128)(2,1)S(1)} custom-call(bf16[3,64,384]{2,1,0:T(8,128)(2,1)S(1)} %bitcast.5, bf16[8,4,256,256]{3,2,1,0:T(8,128)(2,1)S(1)} %bitcast.3, bf16[8,128,128]{2,1,0:T(8,128)(2,1)S(1)} %bitcast.4, s32[4,4]{1,0:T(4,128)S(1)} %copy-done.3, s32[4,32]{1,0:T(4,128)S(1)} %copy-done.4, s32[4,32]{1,0:T(4,128)S(1)} %copy-done.5, ...), custom_call_target="tpu_custom_call" | custom-call | tf_op jit(solution)/shard_map/pallas_call | solution.py:397
  57.0 0.7 %copy.9 = bf16[192,384]{1,0:T(8,128)(2,1)} copy(bf16[192,384]{1,0:T(8,128)(2,1)S(1)} %shard_map.73) | data formatting | bytes 294912
Async XLA Ops:
  0.0 2.2 %copy-start = (bf16[1,1,32,256,256]{4,3,2,1,0:T(8,128)(2,1)S(1)}, bf16[1,1,32,256,256]{4,3,2,1,0:T(8,128)(2,1)}, u32[]{:S(2)}) copy-start(bf16[1,1,32,256,256]{4,3,2,1,0:T(8,128)(2,1)} %param.8) | copy-start | bytes 12582916
  2.2 0.9 %copy-start.1 = (bf16[1,8,128,128]{3,2,1,0:T(8,128)(2,1)S(1)}, bf16[1,8,128,128]{3,2,1,0:T(8,128)(2,1)}, u32[]{:S(2)}) copy-start(bf16[1,8,128,128]{3,2,1,0:T(8,128)(2,1)} %param.9) | copy-start | bytes 786436
  3.1 0.9 %copy-start.2 = (bf16[192,384]{1,0:T(8,128)(2,1)S(1)}, bf16[192,384]{1,0:T(8,128)(2,1)}, u32[]{:S(2)}) copy-start(bf16[192,384]{1,0:T(8,128)(2,1)} %param.7) | copy-start | bytes 442372
  4.0 0.7 %copy-start.3 = (s32[4,4]{1,0:T(4,128)S(1)}, s32[4,4]{1,0:T(4,128)}, u32[]{:S(2)}) copy-start(s32[4,4]{1,0:T(4,128)} %tiles_ref.1) | copy-start | bytes 196
  4.7 0.7 %copy-start.4 = (s32[4,32]{1,0:T(4,128)S(1)}, s32[4,32]{1,0:T(4,128)}, u32[]{:S(2)}) copy-start(s32[4,32]{1,0:T(4,128)} %sector_ref.1) | copy-start | bytes 1540
  5.4 0.7 %copy-start.5 = (s32[4,32]{1,0:T(4,128)S(1)}, s32[4,32]{1,0:T(4,128)}, u32[]{:S(2)}) copy-start(s32[4,32]{1,0:T(4,128)} %term_ref.1) | copy-start | bytes 1540
  6.1 0.7 %copy-start.6 = (s32[1,4,32]{2,1,0:T(4,128)S(1)}, s32[1,4,32]{2,1,0:T(4,128)}, u32[]{:S(2)}) copy-start(s32[1,4,32]{2,1,0:T(4,128)} %live_ref.1) | copy-start | bytes 1540

commit v2 on v1

--- a/solution.py
+++ b/solution.py
@@ -84,7 +84,7 @@
 
 
 MESH = pl.DeviceIdType.MESH
-VMEM_LIMIT = 32 * 1024 * 1024
+VMEM_LIMIT = 60 * 1024 * 1024
 
 
 def place():
@@ -258,9 +258,11 @@
         arrived(step, other)
         apply_home(step)
 
-    def send_side(at):
+    def send_side(at, after=None):
         core_copy(at, True).wait_recv()
         side_out[at] = (part_rows(at, across) + wide(core_buf[1, at])).astype(jnp.bfloat16)
+        if after is not None:
+            side_copy(after).wait_send()
         side_copy(at).start()
 
     def gathered(at):
@@ -322,20 +324,31 @@
     for t in range(1, depth):
         if t + 1 < depth:
             forward(t + 1)
-        if t + 1 == depth - 1:
-            send_side(z)
+        if 2 * t >= depth - 1:
+            @pl.when(jnp.maximum(z, depth - 1 - z) == t)
+            def _():
+                send_side(z)
         for step, there in offsets(t):
             pl.when(there)(functools.partial(finish_home, step))
-    if depth < 3:
-        send_side(z)
+    def send_back(steps_here):
+        last = 0
+        for i, step in enumerate(steps_here):
+            send_side(z + step, z + last)
+            last = step
+            if i == 1:
+                send_z(steps_here[0])
+        side_copy(z + last).wait_send()
+        for step in steps_here[1 if len(steps_here) > 1 else 0:]:
+            send_z(step)
 
     order = []
     for t in range(depth - 1, 0, -1):
         order += offsets(t)[::-1]
-    for step, there in order:
-        pl.when(there)(functools.partial(send_side, z + step))
-    for step, there in order:
-        pl.when(there)(functools.partial(send_z, step))
+    for at_z in range(depth):
+        @pl.when(z == at_z)
+        def _():
+            steps_here = sorted((i - at_z for i in range(depth) if i != at_z), key=lambda i: (-abs(i), -i))
+            send_back(steps_here)
 
     total = gathered(z)
 
@@ -359,7 +372,6 @@
         at = z + step
         core_copy(at, True).wait_send()
         core_copy(at, False).wait_send()
-        side_copy(at).wait_send()
         copy(side, step, o).wait_send()
         copy(core, step, o).wait_send()
         copy(core, step, across).wait_send()
@@ -397,7 +409,7 @@
     return pl.pallas_call(
         functools.partial(whole_kernel, depth),
         out_shape=jax.ShapeDtypeStruct(psi.shape, jnp.bfloat16),
-        in_specs=[pl.BlockSpec(memory_space=pltpu.HBM)] * len(operands),
+        in_specs=[pl.BlockSpec(memory_space=pl.ANY)] * len(operands),
         out_specs=pl.BlockSpec(memory_space=pltpu.VMEM),
         scratch_shapes=[vmem((4 * rows // unit, unit, columns), jnp.bfloat16)] * (2 * depth - 1)
         + [vmem(env.shape, env.dtype), vmem(right.shape, right.dtype)] + ints

time: 58.2 us -> 53.4 us (0.918)
  local copies, waits for them, and re-layouts: 7.43 us -> 1.59 us
  Pallas kernels: 50.2 us -> 51.7 us
    unnamed x15 -> x1, local copies, waits for them, and re-layouts: 7.43 us -> 1.59 us
    pallas_call x1, Pallas kernels: 50.2 us -> 51.7 us  [small_body(): pl.pallas_call(functools.partial(whole_kernel, depth), out_shape=jax.Shap...]
where the time goes in v2:
time: 53.4 us; the launch traced here: 53.3 us
  Pallas kernels  51.7 us (97%)
  local copies, waits for them, and re-layouts  1.59 us (3%)
    pallas_call x1, Pallas kernels, small_body(): pl.pallas_call(functools.partial(whole_kernel, depth), out_shape=jax.Shap...  51.7 us
    unnamed x1, local copies, waits for them, and re-layouts  1.59 us

profile of v2, /device:TPU:0, one launch (start us, length us, event | category | flops | bytes accessed | tf_op | source)
XLA Modules:
  0.0 53.3 jit_solution(8070526886404654421)
XLA Ops:
  0.0 51.7 %shard_map.73 = bf16[192,384]{1,0:T(8,128)(2,1)} custom-call(bf16[3,64,384]{2,1,0:T(8,128)(2,1)} %bitcast.5, bf16[8,4,256,256]{3,2,1,0:T(8,128)(2,1)} %bitcast.3, bf16[8,128,128]{2,1,0:T(8,128)(2,1)} %bitcast.4, s32[4,4]{1,0:T(4,128)} %tiles_ref.1, s32[4,32]{1,0:T(4,128)} %sector_ref.1, s32[4,32]{1,0:T(4,128)} %term_ref.1, s32[1,4,32]{2,1,0:T(4,128)} %live_ref.1), custom_call_target="tpu_custom_call" | custom-call | tf_op jit(solution)/shard_map/pallas_call | solution.py:409
  51.7 1.6 %copy.9 = bf16[192,384]{1,0:T(8,128)(2,1)} copy(bf16[192,384]{1,0:T(8,128)(2,1)} %shard_map.73) | data formatting | bytes 294912

commit v3 on v1

--- a/solution.py
+++ b/solution.py
@@ -84,7 +84,7 @@
 
 
 MESH = pl.DeviceIdType.MESH
-VMEM_LIMIT = 32 * 1024 * 1024
+VMEM_LIMIT = 60 * 1024 * 1024
 
 
 def place():
@@ -127,18 +127,23 @@
     pairs = env.shape[0]
     units, unit = psi_ref.shape[:2]
     rows = units * unit
+    chunk_units = units // CHUNKS
+    chunk_rows = rows // CHUNKS
     per_tile = TILE // unit
     own_tiles = homes[0].shape[0] // per_tile
     sectors = tiles.shape[1]
     up, down, side, core = 0, 1, 2, 3
 
-    def block(step, col):
-        return homes[step + depth - 1].at[pl.ds(col * units, units)]
+    def block(step, col, chunk):
+        return homes[step + depth - 1].at[pl.ds(col * units + chunk * chunk_units, chunk_units)]
+
+    def within(chunk):
+        return pl.ds(chunk * chunk_rows, chunk_rows)
 
     loads = [
         pltpu.make_async_copy(source, target, local_sem.at[i])
         for i, (source, target) in enumerate((
-            (psi_ref, block(0, o)), (tiles_ref, tiles), (sector_ref, sector), (term_ref, term), (live_ref, live),
+            (psi_ref, homes[depth - 1].at[pl.ds(o * units, units)]), (tiles_ref, tiles), (sector_ref, sector), (term_ref, term), (live_ref, live),
             (right_ref, right), (env_ref, env),
         ))
     ]
@@ -146,22 +151,22 @@
         load.start()
     enter(z, across, sibling, depth)
 
-    def copy(way, step, col):
+    def copy(way, step, col, chunk):
         shift = (-1, 1, 0, 0)[way]
         where = ({"task": z + 1}, {"task": z - 1}, {"ops": across}, {"ops": sibling})[way]
-        index = (z + step) * 4 + col
+        index = ((z + step) * 4 + col) * CHUNKS + chunk
         own = step == 0 and col is o
         return pltpu.make_async_remote_copy(
-            src_ref=psi_ref if own else block(step, col),
-            dst_ref=block(step + shift, col),
+            src_ref=psi_ref.at[pl.ds(chunk * chunk_units, chunk_units)] if own else block(step, col, chunk),
+            dst_ref=block(step + shift, col, chunk),
             send_sem=send_sem.at[way, index],
             recv_sem=recv_sem.at[index],
             device_id=where,
             device_id_type=MESH,
         )
 
-    def arrived(step, col):
-        copy(core, step, col).wait_recv()
+    def arrived(step, col, chunk):
+        copy(core, step, col, chunk).wait_recv()
 
     def offsets(t):
         return ((-t, z - t >= 0), (t, z + t <= depth - 1))
@@ -177,22 +182,22 @@
             device_id_type=MESH,
         )
 
-    def side_copy(at):
+    def side_copy(at, chunk):
         return pltpu.make_async_remote_copy(
-            src_ref=side_out.at[at],
-            dst_ref=side_buf.at[at],
-            send_sem=side_send.at[at],
-            recv_sem=side_recv.at[at],
+            src_ref=side_out.at[at, within(chunk)],
+            dst_ref=side_buf.at[at, within(chunk)],
+            send_sem=side_send.at[at, chunk],
+            recv_sem=side_recv.at[at, chunk],
             device_id={"ops": across},
             device_id_type=MESH,
         )
 
-    def z_copy(at, rising):
+    def z_copy(at, rising, chunk):
         return pltpu.make_async_remote_copy(
-            src_ref=z_out.at[at],
-            dst_ref=(up_buf if rising else down_buf).at[at],
-            send_sem=z_send.at[at],
-            recv_sem=(up_recv if rising else down_recv).at[at],
+            src_ref=z_out.at[at, within(chunk)],
+            dst_ref=(up_buf if rising else down_buf).at[at, within(chunk)],
+            send_sem=z_send.at[at, chunk],
+            recv_sem=(up_recv if rising else down_recv).at[at, chunk],
             device_id={"task": z + 1 if rising else z - 1},
             device_id_type=MESH,
         )
@@ -200,8 +205,8 @@
     def wide(value):
         return value.astype(jnp.float32)
 
-    def part_rows(at, col):
-        return wide(part[at, pl.ds(pl.multiple_of(col * rows, 16), rows), :])
+    def part_rows(at, col, chunk):
+        return wide(part[at, pl.ds(pl.multiple_of(col * rows + chunk * chunk_rows, 16), chunk_rows), :])
 
     def apply_home(step):
         home = z + step
@@ -252,21 +257,27 @@
         core_copy(home, False).start()
 
     def finish_home(step):
-        arrived(step, across)
-        copy(core, step, across).start()
-        arrived(step, sibling)
-        arrived(step, other)
+        for chunk in range(CHUNKS):
+            arrived(step, across, chunk)
+            copy(core, step, across, chunk).start()
+        for chunk in range(CHUNKS):
+            arrived(step, sibling, chunk)
+            arrived(step, other, chunk)
         apply_home(step)
 
     def send_side(at):
         core_copy(at, True).wait_recv()
-        side_out[at] = (part_rows(at, across) + wide(core_buf[1, at])).astype(jnp.bfloat16)
-        side_copy(at).start()
-
-    def gathered(at):
-        core_copy(at, False).wait_recv()
-        side_copy(at).wait_recv()
-        return part_rows(at, o) + wide(core_buf[0, at]) + wide(side_buf[at])
+        for chunk in range(CHUNKS):
+            side_out[at, within(chunk), :] = (
+                part_rows(at, across, chunk) + wide(core_buf[1, at, within(chunk), :])
+            ).astype(jnp.bfloat16)
+            side_copy(at, chunk).start()
+
+    def gathered(at, chunk):
+        if chunk == 0:
+            core_copy(at, False).wait_recv()
+        side_copy(at, chunk).wait_recv()
+        return part_rows(at, o, chunk) + wide(core_buf[0, at, within(chunk), :]) + wide(side_buf[at, within(chunk), :])
 
     def send_z(step):
         at = z + step
@@ -276,44 +287,48 @@
 
         @pl.when(first)
         def _():
-            z_out[at] = gathered(at).astype(jnp.bfloat16)
+            for chunk in range(CHUNKS):
+                z_out[at, within(chunk), :] = gathered(at, chunk).astype(jnp.bfloat16)
+                z_copy(at, rising, chunk).start()
 
         @pl.when(jnp.logical_not(first))
         def _():
-            total = gathered(at)
-            z_copy(at, rising).wait_recv()
-            z_out[at] = (total + wide(buf[at])).astype(jnp.bfloat16)
-
-        z_copy(at, rising).start()
-
-    @pl.when(z < depth - 1)
-    def _():
-        copy(up, 0, o).start()
-
-    @pl.when(z > 0)
-    def _():
-        copy(down, 0, o).start()
-
-    copy(side, 0, o).start()
-    copy(core, 0, o).start()
+            for chunk in range(CHUNKS):
+                total = gathered(at, chunk)
+                z_copy(at, rising, chunk).wait_recv()
+                z_out[at, within(chunk), :] = (total + wide(buf[at, within(chunk), :])).astype(jnp.bfloat16)
+                z_copy(at, rising, chunk).start()
+
+    for chunk in range(CHUNKS):
+        @pl.when(z < depth - 1)
+        def _():
+            copy(up, 0, o, chunk).start()
+
+        @pl.when(z > 0)
+        def _():
+            copy(down, 0, o, chunk).start()
+
+        copy(side, 0, o, chunk).start()
+        copy(core, 0, o, chunk).start()
 
     def forward(t):
-        for step, there in offsets(t):
-            @pl.when(there)
-            def _():
-                arrived(step, o)
-
-                if 1 - depth < step < 0:
-                    @pl.when(z < depth - 1)
-                    def _():
-                        copy(up, step, o).start()
-                if 0 < step < depth - 1:
-                    @pl.when(z > 0)
-                    def _():
-                        copy(down, step, o).start()
-
-                copy(side, step, o).start()
-                copy(core, step, o).start()
+        for chunk in range(CHUNKS):
+            for step, there in offsets(t):
+                @pl.when(there)
+                def _():
+                    arrived(step, o, chunk)
+
+                    if 1 - depth < step < 0:
+                        @pl.when(z < depth - 1)
+                        def _():
+                            copy(up, step, o, chunk).start()
+                    if 0 < step < depth - 1:
+                        @pl.when(z > 0)
+                        def _():
+                            copy(down, step, o, chunk).start()
+
+                    copy(side, step, o, chunk).start()
+                    copy(core, step, o, chunk).start()
 
     forward(1)
     for load in loads:
@@ -322,13 +337,12 @@
     for t in range(1, depth):
         if t + 1 < depth:
             forward(t + 1)
-        if t + 1 == depth - 1:
-            send_side(z)
+        if 2 * t >= depth - 1:
+            @pl.when(jnp.maximum(z, depth - 1 - z) == t)
+            def _():
+                send_side(z)
         for step, there in offsets(t):
             pl.when(there)(functools.partial(finish_home, step))
-    if depth < 3:
-        send_side(z)
-
     order = []
     for t in range(depth - 1, 0, -1):
         order += offsets(t)[::-1]
@@ -337,42 +351,43 @@
     for step, there in order:
         pl.when(there)(functools.partial(send_z, step))
 
-    total = gathered(z)
-
-    @pl.when(z == 0)
-    def _():
-        z_copy(z, False).wait_recv()
-        out_ref[...] = (total + wide(down_buf[z])).astype(jnp.bfloat16)
-
-    @pl.when(z == depth - 1)
-    def _():
-        z_copy(z, True).wait_recv()
-        out_ref[...] = (total + wide(up_buf[z])).astype(jnp.bfloat16)
-
-    @pl.when((z > 0) & (z < depth - 1))
-    def _():
-        z_copy(z, True).wait_recv()
-        z_copy(z, False).wait_recv()
-        out_ref[...] = (total + wide(up_buf[z]) + wide(down_buf[z])).astype(jnp.bfloat16)
+    def finish(chunk, below, above):
+        total = gathered(z, chunk)
+        if below:
+            z_copy(z, True, chunk).wait_recv()
+            total += wide(up_buf[z, within(chunk), :])
+        if above:
+            z_copy(z, False, chunk).wait_recv()
+            total += wide(down_buf[z, within(chunk), :])
+        out_ref[within(chunk), :] = total.astype(jnp.bfloat16)
+
+    for below, above, here in (
+        (False, True, z == 0), (True, False, z == depth - 1), (True, True, (z > 0) & (z < depth - 1))
+    ):
+        @pl.when(here)
+        def _():
+            for chunk in range(CHUNKS):
+                finish(chunk, below, above)
 
     def drain(step):
         at = z + step
         core_copy(at, True).wait_send()
         core_copy(at, False).wait_send()
-        side_copy(at).wait_send()
-        copy(side, step, o).wait_send()
-        copy(core, step, o).wait_send()
-        copy(core, step, across).wait_send()
-        if step != 0:
-            z_copy(at, step > 0).wait_send()
-        if 1 - depth < step <= 0:
-            @pl.when(z < depth - 1)
-            def _():
-                copy(up, step, o).wait_send()
-        if 0 <= step < depth - 1:
-            @pl.when(z > 0)
-            def _():
-                copy(down, step, o).wait_send()
+        for chunk in range(CHUNKS):
+            side_copy(at, chunk).wait_send()
+            copy(side, step, o, chunk).wait_send()
+            copy(core, step, o, chunk).wait_send()
+            copy(core, step, across, chunk).wait_send()
+            if step != 0:
+                z_copy(at, step > 0, chunk).wait_send()
+            if 1 - depth < step <= 0:
+                @pl.when(z < depth - 1)
+                def _():
+                    copy(up, step, o, chunk).wait_send()
+            if 0 <= step < depth - 1:
+                @pl.when(z > 0)
+                def _():
+                    copy(down, step, o, chunk).wait_send()
 
     drain(0)
     for step, there in order:
@@ -380,6 +395,7 @@
 
 
 UNROLL = 2
+CHUNKS = 2
 
 
 def small_body(psi, left_env, right_env, sec_tiles, task_sector, task_term, task_live):
@@ -389,7 +405,7 @@
     env = left_env.reshape(-1, depth, span, span)
     right = right_env[0]
     pairs = env.shape[0]
-    unit = math.gcd(rows, TILE)
+    unit = math.gcd(rows // CHUNKS, TILE)
     operands = (psi.reshape(-1, unit, columns), env, right, sec_tiles, task_sector, task_term, task_live)
     dma, vmem, smem = pltpu.SemaphoreType.DMA, pltpu.VMEM, pltpu.SMEM
     blocks = vmem((depth, rows, columns), jnp.bfloat16)
@@ -397,15 +413,15 @@
     return pl.pallas_call(
         functools.partial(whole_kernel, depth),
         out_shape=jax.ShapeDtypeStruct(psi.shape, jnp.bfloat16),
-        in_specs=[pl.BlockSpec(memory_space=pltpu.HBM)] * len(operands),
+        in_specs=[pl.BlockSpec(memory_space=pl.ANY)] * len(operands),
         out_specs=pl.BlockSpec(memory_space=pltpu.VMEM),
         scratch_shapes=[vmem((4 * rows // unit, unit, columns), jnp.bfloat16)] * (2 * depth - 1)
         + [vmem(env.shape, env.dtype), vmem(right.shape, right.dtype)] + ints
         + [smem((pairs,), jnp.int32)] * 2
         + [vmem((pairs, span // TILE, TILE, columns), jnp.bfloat16), vmem((depth, 4 * rows, columns), jnp.bfloat16),
            vmem((2, depth, rows, columns), jnp.bfloat16)] + [blocks] * 5
-        + [dma((4, depth * 4)), dma((depth * 4,)), dma((len(operands),)), dma((2, depth)), dma((depth,)),
-           dma((depth,)), dma((2, depth)), dma((depth,)), dma((depth,)), dma((depth,))],
+        + [dma((4, depth * 4 * CHUNKS)), dma((depth * 4 * CHUNKS,)), dma((len(operands),)), dma((2, depth))]
+        + [dma((depth, CHUNKS))] * 2 + [dma((2, depth))] + [dma((depth, CHUNKS))] * 3,
         compiler_params=pltpu.CompilerParams(
             collective_id=0, has_side_effects=True, vmem_limit_bytes=VMEM_LIMIT
         ),

time: 58.2 us -> 51 us (0.88)
  local copies, waits for them, and re-layouts: 7.43 us -> 1.59 us
  Pallas kernels: 50.2 us -> 49.3 us
    unnamed x15 -> x1, local copies, waits for them, and re-layouts: 7.43 us -> 1.59 us
    pallas_call x1, Pallas kernels: 50.2 us -> 49.3 us  [small_body(): pl.pallas_call(functools.partial(whole_kernel, depth), out_shape=jax.Shap...]
where the time goes in v3:
time: 51 us; the launch traced here: 50.9 us
  Pallas kernels  49.3 us (97%)
  local copies, waits for them, and re-layouts  1.59 us (3%)
    pallas_call x1, Pallas kernels, small_body(): pl.pallas_call(functools.partial(whole_kernel, depth), out_shape=jax.Shap...  49.3 us
    unnamed x1, local copies, waits for them, and re-layouts  1.59 us

profile of v3, /device:TPU:0, one launch (start us, length us, event | category | flops | bytes accessed | tf_op | source)
XLA Modules:
  0.0 50.9 jit_solution(16336505534430704353)
XLA Ops:
  0.0 49.3 %shard_map.73 = bf16[192,384]{1,0:T(8,128)(2,1)} custom-call(bf16[6,32,384]{2,1,0:T(8,128)(2,1)} %bitcast.5, bf16[8,4,256,256]{3,2,1,0:T(8,128)(2,1)} %bitcast.3, bf16[8,128,128]{2,1,0:T(8,128)(2,1)} %bitcast.4, s32[4,4]{1,0:T(4,128)} %tiles_ref.1, s32[4,32]{1,0:T(4,128)} %sector_ref.1, s32[4,32]{1,0:T(4,128)} %term_ref.1, s32[1,4,32]{2,1,0:T(4,128)} %live_ref.1), custom_call_target="tpu_custom_call" | custom-call | tf_op jit(solution)/shard_map/pallas_call | solution.py:413
  49.3 1.6 %copy.9 = bf16[192,384]{1,0:T(8,128)(2,1)} copy(bf16[192,384]{1,0:T(8,128)(2,1)} %shard_map.73) | data formatting | bytes 294912

commit v4 on v3

--- a/solution.py
+++ b/solution.py
@@ -124,7 +124,7 @@
      core_recv, side_recv, up_recv, down_recv) = scratch
     z, o, across, sibling = place()
     other = lax.rem(sibling + 2, 4)
-    pairs = env.shape[0]
+    pairs, span = env.shape[0], env.shape[-1]
     units, unit = psi_ref.shape[:2]
     rows = units * unit
     chunk_units = units // CHUNKS
@@ -229,13 +229,12 @@
             rows_in = jnp.concatenate(pieces, axis=0)
             turned = jnp.dot(env[pair, home], rows_in, preferred_element_type=jnp.float32).astype(jnp.bfloat16)
             chosen = right[term[z, slot]]
+            stacked = jnp.concatenate([turned[:, v * MR:(v + 1) * MR] for v in range(NV)], axis=0)
+            result = jnp.dot(stacked, chosen, preferred_element_type=jnp.float32).astype(jnp.bfloat16)
             for v in range(NV):
-                cols = slice(v * MR, (v + 1) * MR)
-                result = jnp.dot(
-                    turned[:, cols], chosen, preferred_element_type=jnp.float32
-                ).astype(jnp.bfloat16)
-                mixed[pair, 0, :, cols] = result[:TILE]
-                mixed[pair, 1, :, cols] = result[TILE:]
+                for half in range(span // TILE):
+                    at_row = v * span + half * TILE
+                    mixed[pair, half, :, v * MR:(v + 1) * MR] = result[at_row:at_row + TILE]
             return 0
 
         lax.fori_loop(0, pairs, one_slot, 0, unroll=UNROLL)
@@ -394,7 +393,7 @@
         pl.when(there)(functools.partial(drain, step))
 
 
-UNROLL = 2
+UNROLL = 4
 CHUNKS = 2
 
 

time: 51 us -> 49.7 us (0.975)
  Pallas kernels: 49.3 us -> 48 us
    pallas_call x1, Pallas kernels: 49.3 us -> 48 us  [small_body(): pl.pallas_call(functools.partial(whole_kernel, depth), out_shape=jax.Shap...]
where the time goes in v4:
time: 49.7 us; the launch traced here: 49.6 us
  Pallas kernels  48 us (97%)
  local copies, waits for them, and re-layouts  1.59 us (3%)
    pallas_call x1, Pallas kernels, small_body(): pl.pallas_call(functools.partial(whole_kernel, depth), out_shape=jax.Shap...  48 us
    unnamed x1, local copies, waits for them, and re-layouts  1.59 us

profile of v4, /device:TPU:0, one launch (start us, length us, event | category | flops | bytes accessed | tf_op | source)
XLA Modules:
  0.0 49.6 jit_solution(18341775055249642367)
XLA Ops:
  0.0 48.0 %shard_map.73 = bf16[192,384]{1,0:T(8,128)(2,1)} custom-call(bf16[6,32,384]{2,1,0:T(8,128)(2,1)} %bitcast.5, bf16[8,4,256,256]{3,2,1,0:T(8,128)(2,1)} %bitcast.3, bf16[8,128,128]{2,1,0:T(8,128)(2,1)} %bitcast.4, s32[4,4]{1,0:T(4,128)} %tiles_ref.1, s32[4,32]{1,0:T(4,128)} %sector_ref.1, s32[4,32]{1,0:T(4,128)} %term_ref.1, s32[1,4,32]{2,1,0:T(4,128)} %live_ref.1), custom_call_target="tpu_custom_call" | custom-call | tf_op jit(solution)/shard_map/pallas_call | solution.py:412
  48.0 1.6 %copy.9 = bf16[192,384]{1,0:T(8,128)(2,1)} copy(bf16[192,384]{1,0:T(8,128)(2,1)} %shard_map.73) | data formatting | bytes 294912
